TPU v7x, 256 devices: a whole 4x4x8 slice. The times are simulated.
256 devices in a mesh: ctx: 32 (over x, z), tp: 8 (over y, core).
Axes of the slice: x: 4, y: 4, z: 8, core: 2. Of those that a mesh axis runs over, the one named last changes fastest.
Arguments:
- queries: bfloat16 [4096, 8192], P('ctx', 'tp'), may hold values from -160 to 160
- key_rows: bfloat16 [4096, 1024], P('ctx', 'tp'), may hold values from -4.5 to 4.5
- value_rows: bfloat16 [4096, 1024], P('ctx', 'tp'), may hold values from -6 to 6
- doc_lengths: int32 [16], replicated, may hold values from 1 to 2112, 4096 in all
- gate_input: bfloat16 [4096, 8192], P('ctx', 'tp'), may hold values from -6 to 6
- bc_input: bfloat16 [4096, 2, 4, 256], P('ctx'), may hold values from -1.796875 to 1.796875
- step_size: float32 [4096, 128], P('ctx', 'tp'), may hold values from 0.5 to 2
- decay_rate: float32 [128], P('tp'), may hold values from 0 to 1, as said below
- skip_gain: float32 [128], P('tp'), may hold values from 1 to 4
- conv_x: float32 [4, 8192], P(None, 'tp'), may hold values from -3 to 3
- conv_bc: float32 [4, 2, 4, 256], replicated, may hold values from -3 to 3
- norm_gain: float32 [8192], P('tp'), may hold values from 0.1 to 1.9
Outputs:
- mixed: bfloat16 [4096, 8192], P('ctx', 'tp')
Inputs may be any that keep to these rules, and one draw needn't show every extreme that they name: `doc_lengths`: documents lie end to end in token order; the longest has exactly 2112 tokens. `decay_rate`: positive rates.
All inputs are finite; a program needn't handle non-finite values.
Results may differ from a plain program's by a relative error of at most 0.02.
Values may be sent and summed in bfloat16 or wider, within the bound.
No kernel may reach another device: no remote copies, remote signals or barrier semaphores. Data moves between devices by JAX's collectives and lax.ppermute only.
A program may use at most 128 MiB of HBM per device.

v0:
```python
import math

import jax
import jax.numpy as jnp
from jax import lax
from jax.sharding import PartitionSpec as P

EPSILON = 1e-05
NEGATIVE_FILL = -1e30


def from_behind(x, axis, by):
    size = lax.axis_size(axis)
    pairs = [(i, i + by) for i in range(size) if 0 <= i + by < size]
    return lax.ppermute(x, axis, pairs)


def prefix(x, axis, combine, identity):
    size, mine = (lax.axis_size(axis), lax.axis_index(axis))
    everything = jax.tree.map(
        lambda part, kind: lax.all_gather(part.astype(kind), axis), x, (jnp.bfloat16, jnp.bfloat16)
    )
    start = jax.tree.map(
        lambda part, zero: jnp.broadcast_to(jnp.asarray(zero, part.dtype), part.shape), x, identity
    )

    def step(k, before):
        reached = k < mine
        new = combine(
            before, jax.tree.map(lambda part, own: part[k].astype(own.dtype), everything, x)
        )
        return jax.tree.map(lambda a, b: jnp.where(reached, a, b), new, before)

    return lax.fori_loop(0, size, step, start)


def swapped(block, axis, bit):
    count = lax.axis_size(axis)
    route = []
    for low in range(count):
        high = low | 1 << bit
        if high != low and high < count:
            route += [(low, high), (high, low)]
    return lax.ppermute(block, axis, route)


def first_positions(doc_lengths, positions):
    doc_ends = jnp.cumsum(doc_lengths)
    doc_starts = doc_ends - doc_lengths
    covered = doc_starts[None, :] <= positions[:, None]
    return jnp.max(
        jnp.where(covered, doc_starts[None, :], jnp.zeros_like(doc_starts)[None, :]), axis=1
    )


def attend(
    running, key_block, value_block, key_start, query_rows, query_pos, query_first, score_scale
):
    maximum, totals, summed = running
    key_pos = key_start + jnp.arange(key_block.shape[0], dtype=jnp.int32)
    scores = (
        jnp.einsum("qhd,kd->hqk", query_rows, key_block, preferred_element_type=jnp.float32)
        * score_scale
    )
    visible = (
        (key_pos[None, :] <= query_pos[:, None]) & (key_pos[None, :] >= query_first[:, None])
    )[None]
    masked = jnp.where(visible, scores, NEGATIVE_FILL)
    new_maximum = jnp.maximum(maximum, jnp.max(masked, axis=-1))
    exponent = jnp.where(visible, jnp.exp(masked - new_maximum[..., None]), 0.0)
    factor = jnp.exp(maximum - new_maximum)
    totals = totals * factor + jnp.sum(exponent, axis=-1)
    weights = exponent.astype(jnp.bfloat16)
    summed = summed * factor[..., None] + jnp.einsum(
        "hqk,kd->hqd", weights, value_block, preferred_element_type=jnp.float32
    )
    return (new_maximum, totals, summed)


def key_folder(query_rows, query_pos, query_first, score_scale):
    query_last = jnp.max(query_pos)
    earliest = jnp.min(query_first)

    def maybe_attend(running, key_slab, value_slab, key_start):
        needed = (key_start <= query_last) & (key_start + key_slab.shape[0] > earliest)

        def compute(inner_run):
            return attend(
                inner_run,
                key_slab,
                value_slab,
                key_start,
                query_rows,
                query_pos,
                query_first,
                score_scale,
            )

        def keep(inner_run):
            return inner_run

        return lax.cond(needed, compute, keep, running)

    def fold_keys(running, pieces, offset):
        key_block, value_block = pieces
        key_count = key_block.shape[0]
        block_width = 256
        block_count = key_count // block_width

        def visit(inner_run, entries):
            block_index, key_slab, value_slab = entries
            return (maybe_attend(inner_run, key_slab, value_slab, block_index * block_width), None)

        running, _ = lax.scan(
            visit,
            running,
            (
                jnp.arange(block_count, dtype=jnp.int32),
                key_block.reshape(block_count, block_width, -1),
                value_block.reshape(block_count, block_width, -1),
            ),
        )
        return running

    return fold_keys


def finish(running, row_count):
    maximum, totals, summed = running
    output = summed / totals[..., None]
    return jnp.transpose(output, (1, 0, 2)).reshape(row_count, -1).astype(jnp.bfloat16)


def causal_local(extended, taps, positions, first_token, tap_count):
    row_count = positions.shape[0]
    accumulated = jnp.zeros((row_count,) + extended.shape[1:], jnp.float32)
    for shift_by in range(tap_count):
        tap_rows = extended[tap_count - 1 - shift_by : tap_count - 1 - shift_by + row_count].astype(
            jnp.float32
        )
        usable = (positions - shift_by >= first_token).reshape(
            (row_count,) + (1,) * (extended.ndim - 1)
        )
        accumulated = accumulated + jnp.where(
            usable, tap_rows * taps[tap_count - 1 - shift_by], 0.0
        )
    return accumulated


def combine_states(earlier, following):
    return (earlier[0] * following[0], earlier[1] * following[0][:, None, None] + following[1])


def on_device(
    queries,
    key_rows,
    value_rows,
    doc_lengths,
    gate_input,
    bc_input,
    step_size,
    decay_rate,
    skip_gain,
    conv_x,
    conv_bc,
    norm_gain,
):
    row_count = queries.shape[0]
    head_size = key_rows.shape[1]
    head_count = queries.shape[1] // head_size
    score_scale = 1.0 / math.sqrt(head_size)
    ctx_index = lax.axis_index("ctx")
    block_start = ctx_index * row_count
    own_pos = block_start + jnp.arange(row_count, dtype=jnp.int32)
    own_first = first_positions(doc_lengths, own_pos)
    initial = (
        jnp.full((head_count, row_count), NEGATIVE_FILL, jnp.float32),
        jnp.zeros((head_count, row_count), jnp.float32),
        jnp.zeros((head_count, row_count, head_size), jnp.float32),
    )
    query_rows = queries.reshape(row_count, head_count, head_size)
    running = key_folder(query_rows, own_pos, own_first, score_scale)(
        initial,
        (
            lax.all_gather(key_rows, "ctx", axis=0, tiled=True),
            lax.all_gather(value_rows, "ctx", axis=0, tiled=True),
        ),
        jnp.int32(0),
    )
    attended = finish(running, row_count)
    group_index = lax.axis_index("tp") // 2
    bc_local = lax.dynamic_index_in_dim(bc_input, group_index, 2, keepdims=False)
    conv_bc_local = lax.dynamic_index_in_dim(conv_bc, group_index, 2, keepdims=False)
    tap_count = conv_x.shape[0]
    rim_input, rim_bc = from_behind(
        (attended[row_count - tap_count + 1 :], bc_local[row_count - tap_count + 1 :]), "ctx", 1
    )
    mixed_input = jax.nn.silu(
        causal_local(
            jnp.concatenate([rim_input, attended], 0), conv_x, own_pos, own_first, tap_count
        )
    ).astype(jnp.bfloat16)
    bc_conv = jax.nn.silu(
        causal_local(
            jnp.concatenate([rim_bc, bc_local], 0), conv_bc_local, own_pos, own_first, tap_count
        )
    ).astype(jnp.bfloat16)
    heads_local = step_size.shape[1]
    input_heads = mixed_input.reshape(row_count, heads_local, -1)
    b_values = bc_conv[:, 0]
    c_values = bc_conv[:, 1]
    highest = lax.Precision.HIGHEST
    log_decay = -decay_rate[None, :] * step_size
    cumulated = jnp.cumsum(log_decay, axis=0)
    gram_matrix = jnp.dot(c_values, b_values.T, preferred_element_type=jnp.float32)
    visible = (own_pos[None, :] >= own_first[:, None]) & (own_pos[None, :] <= own_pos[:, None])
    cum_heads = cumulated.T
    log_gap = jnp.where(visible[None], cum_heads[:, :, None] - cum_heads[:, None, :], -jnp.inf)
    mixing = gram_matrix[None] * jnp.exp(log_gap) * step_size.T[:, None, :]
    input_wide = input_heads.astype(jnp.float32)
    inner_part = jnp.einsum("hts,shp->thp", mixing, input_wide, precision=highest)
    last_start = own_first[-1]
    state_weight = jnp.where(
        (own_pos >= last_start)[:, None], jnp.exp(cumulated[-1][None, :] - cumulated), 0.0
    )
    state_weight = state_weight * step_size
    block_state = jnp.einsum(
        "shp,sn->hpn",
        state_weight[:, :, None] * input_wide,
        b_values.astype(jnp.float32),
        precision=highest,
    )
    carry_decay = jnp.where(last_start < block_start, jnp.exp(cumulated[-1]), 0.0)
    identity = (jnp.ones_like(carry_decay), jnp.zeros_like(block_state))
    _, incoming = prefix((carry_decay, block_state), "ctx", combine_states, identity)
    carry_in = (own_first < block_start).astype(jnp.float32)
    carried_part = jnp.einsum(
        "tn,hpn->thp", c_values.astype(jnp.float32), incoming, precision=highest
    )
    carried_part = carried_part * (jnp.exp(cumulated) * carry_in[:, None])[:, :, None]
    ssm_out = inner_part + carried_part + skip_gain[None, :, None] * input_wide
    gated = ssm_out.reshape(row_count, -1) * jax.nn.silu(gate_input.astype(jnp.float32))
    square_sum = jnp.sum(gated * gated, axis=1)
    partner_sum = swapped(square_sum, "tp", 0)
    mean_square = (square_sum + partner_sum) / (2 * gated.shape[1])
    return (gated * lax.rsqrt(mean_square + EPSILON)[:, None] * norm_gain[None, :]).astype(
        jnp.bfloat16
    )


def solution(mesh):
    return jax.shard_map(
        on_device,
        mesh=mesh,
        in_specs=(
            P("ctx", "tp"),
            P("ctx", "tp"),
            P("ctx", "tp"),
            P(),
            P("ctx", "tp"),
            P("ctx", None, None, None),
            P("ctx", "tp"),
            P("tp"),
            P("tp"),
            P(None, "tp"),
            P(),
            P("tp"),
        ),
        out_specs=P("ctx", "tp"),
        check_vma=False,
    )
```

profile of v0, /device:TPU:1, one launch (start us, length us, event | category | flops | bytes accessed | tf_op | source)
XLA Modules:
  0.0 433.5 jit_solution(2388203920477251056)
XLA Ops:
  6.5 0.7 all-gather.6.cloned.1.call-update
  7.3 0.7 all-gather.8.cloned.1.call-update
  8.4 4.4 %collective-permute-start.1 = (bf16[3,2,256]{2,0,1:T(4,128)(2,1)S(1)}, bf16[3,2,256]{2,0,1:T(4,128)(2,1)S(1)}, u32[]{:S(2)}, u32[]{:S(2)}) collective-permute-start(bf16[3,2,256]{2,0,1:T(4,128)(2,1)S(1)} %slice_bitcast_fusion), channel_id=1, source_target_pairs={{0,8},{8,16},{16,24},{24,32},{32,40},{40,48},{48,56},{56,64},{64,7... | collective-permute-start | bytes 9224 | tf_op jit(solution)/shard_map/ppermute | solution.py:15
  12.8 0.7 copy.77
  13.7 0.7 sub.59
  15.1 0.7 slice.91
  15.8 0.7 reduce_min.9
  16.5 1.1 copy.78
  18.4 0.7 neg.17
  19.1 0.8 broadcast_multiply_fusion
  20.2 0.7 broadcast_compare_fusion
  20.8 0.8 constant_dynamic-slice_fusion.2
  21.7 0.8 select_multiply_fusion
  22.4 0.9 fusion.55
  23.3 62.2 %all-gather.6.cloned.1.call-done = bf16[4096,128]{1,0:T(8,128)(2,1)} async-done(((bf16[128,128]{1,0:T(8,128)(2,1)}), bf16[4096,128]{1,0:T(8,128)(2,1)}) %all-gather.6.cloned.1.call-update) | async-done | bytes 1048592 | tf_op jit(solution)/shard_map/all_gather | solution.py:185
  85.5 76.4 %all-gather.8.cloned.1.call-done = bf16[4096,128]{1,0:T(8,128)(2,1)} async-done(((bf16[128,128]{1,0:T(8,128)(2,1)}), bf16[4096,128]{1,0:T(8,128)(2,1)}) %all-gather.8.cloned.1.call-update) | async-done | bytes 1048592 | tf_op jit(solution)/shard_map/all_gather | solution.py:186
  162.0 43.8 %while.29 = (s32[]{:T(128)}, f32[8,128]{1,0:T(8,128)S(1)}, f32[8,128]{1,0:T(8,128)S(1)}, f32[8,128,128]{2,1,0:T(8,128)S(1)}, s32[16]{0:T(128)S(1)}, /*index=5*/s...) while((s32[]{:T(128)}, f32[8,128]{1,0:T(8,128)S(1)}, ...), condition=%wide.region_9.10_spmd.clone, body=%wide.region_4.9_spmd.clone.sunk | while | flops 136939904 | bytes 4790115 | solution.py:114
  164.5 2.9 conditional.3
  164.6 1.2 fusion.54
  166.0 1.3 convolution_add_fusion
  172.5 0.6 dynamic_slice.64
  206.3 1.9 collective-permute-start
  208.6 2.8 collective-permute-done
  211.4 1.1 bitcast_multiply_fusion
  212.5 1.4 convolution_convert_fusion
  213.9 52.3 %all-gather.1 = bf16[32,1,16]{2,1,0:T(2,128)(2,1)S(1)} all-gather(bf16[1,1,16]{2,1,0:T(2,128)(2,1)S(1)} %get-tuple-element.414), channel_id=1, replica_groups=mesh['ctx'=32,'tp'=8] {'ctx'}, dimensions={0}, use_global_device_ids=true | all-gather | bytes 1056 | tf_op jit(solution)/shard_map/all_gather | solution.py:21
  266.9 1.3 convolution_bitcast_fusion
  268.2 112.2 %all-gather.10.cloned.1.call-done = bf16[512,64,256]{2,1,0:T(8,128)(2,1)} async-done(((bf16[16,64,256]{2,1,0:T(8,128)(2,1)}), bf16[512,64,256]{2,1,0:T(8,128)(2,1)}) %all-gather.10.cloned.1.call-update) | async-done | bytes 16777232 | tf_op jit(solution)/shard_map/all_gather | solution.py:21
  380.4 42.7 %while.30 = (s32[]{:T(128)}, f32[16,64,256]{2,1,0:T(8,128)S(1)}, s32[]{:T(128)}, bf16[32,16]{1,0:T(8,128)(2,1)S(1)}, bf16[32,16,64,256]{3,2,1,0:T(8,128)(2,1)}, /*index=5*/s32[]{:T(128)}, s32[]{:T(128)}) while((s32[]{:T(128)}, f32[16,64,256]{2,1,0:T(8,128)S(1)}, s32[]{:T(128)}, bf16[32,16]{1,0:T(8,128)(2,1)S(1)}, ...), condition=%wide.region_12.13_spmd.clone, body=%wide.region_11.12_spmd.clone.sunk | while | flops 1310740 | bytes 2621705 | solution.py:34
  380.5 1.3 fusion.61
  381.8 1.3 fusion.61
  383.1 1.3 fusion.61
  384.5 1.3 fusion.61
  385.8 1.3 fusion.61
  387.1 1.3 fusion.61
  388.5 1.3 fusion.61
  389.8 1.3 fusion.61
  391.1 1.3 fusion.61
  392.5 1.3 fusion.61
  393.8 1.3 fusion.61
  395.1 1.3 fusion.61
  396.5 1.3 fusion.61
  397.8 1.3 fusion.61
  399.1 1.3 fusion.61
  400.5 1.3 fusion.61
  401.8 1.3 fusion.61
  403.1 1.3 fusion.61
  404.5 1.3 fusion.61
  405.8 1.3 fusion.61
  407.1 1.3 fusion.61
  408.5 1.3 fusion.61
  409.8 1.3 fusion.61
  411.1 1.3 fusion.61
  412.5 1.3 fusion.61
  413.8 1.3 fusion.61
  415.1 1.3 fusion.61
  416.5 1.3 fusion.61
  417.8 1.3 fusion.61
  419.1 1.3 fusion.61
  420.5 1.3 fusion.61
  421.8 1.3 fusion.61
  423.9 1.1 collective-permute-start.2
  425.1 0.8 collective-permute-done.2
  426.1 0.8 copy.91
  (138 shorter events, 15.0 us)
Async XLA Ops:
  6.5 1.5 copy-start
  6.5 259.9 %copy-start.1 = (bf16[128,1024]{1,0:T(8,128)(2,1)S(1)}, bf16[128,1024]{1,0:T(8,128)(2,1)}, u32[]{:S(2)}) copy-start(bf16[128,1024]{1,0:T(8,128)(2,1)} %param.22) | copy-start | bytes 786436
  6.5 79.0 %all-gather.6.cloned.1.call-start = ((), (), s32[]{:S(2)}) async-start(), calls=%async_computation | async-start | bytes 1081344 | tf_op jit(solution)/shard_map/all_gather | solution.py:185
  7.3 154.6 %all-gather.8.cloned.1.call-start = ((), (), s32[]{:S(2)}) async-start(), calls=%async_computation.1 | async-start | bytes 1081344 | tf_op jit(solution)/shard_map/all_gather | solution.py:186
  8.0 372.4 %all-gather.10.cloned.1.call-start = ((), (), s32[]{:S(2)}) async-start(), calls=%async_computation.2 | async-start | bytes 17301504 | tf_op jit(solution)/shard_map/all_gather | solution.py:21
  8.4 258.5 %copy-start.2 = (f32[128,16]{0,1:T(8,128)S(1)}, f32[128,16]{0,1:T(8,128)}, u32[]{:S(2)}) copy-start(f32[128,16]{0,1:T(8,128)} %param.24) | copy-start | bytes 24580
  8.4 199.7 %collective-permute-start.1 = (bf16[3,2,256]{2,0,1:T(4,128)(2,1)S(1)}, bf16[3,2,256]{2,0,1:T(4,128)(2,1)S(1)}, u32[]{:S(2)}, u32[]{:S(2)}) collective-permute-start(bf16[3,2,256]{2,0,1:T(4,128)(2,1)S(1)} %slice_bitcast_fusion), channel_id=1, source_target_pairs={{0,8},{8,16},{16,24},{24,32},{32,40},{40,48},{48,56},{56,64},{64,7... | collective-permute-start | bytes 9224 | tf_op jit(solution)/shard_map/ppermute | solution.py:15
  161.9 261.2 %copy-start.4 = (f32[16]{0:T(128)S(1)}, f32[16]{0:T(128)}, u32[]{:S(2)}) copy-start(f32[16]{0:T(128)} %param.26) | copy-start | bytes 196
  205.8 220.1 %copy-start.3 = (f32[1024]{0:T(1024)S(1)}, f32[1024]{0:T(1024)}, u32[]{:S(2)}) copy-start(f32[1024]{0:T(1024)} %param.29) | copy-start | bytes 12292
  206.3 5.2 %collective-permute-start = (bf16[3,1024]{0,1:T(8,128)(2,1)S(1)}, bf16[3,1024]{0,1:T(8,128)(2,1)S(1)}, u32[]{:S(2)}, u32[]{:S(2)}) collective-permute-start(bf16[3,1024]{0,1:T(8,128)(2,1)S(1)} %bitcast.100), channel_id=1, source_target_pairs={{0,8},{8,16},{16,24},{24,32},{32,40},{40,48},{48,56},{56,64},{64,7... | collective-permute-start | bytes 18440 | tf_op jit(solution)/shard_map/ppermute | solution.py:15
  423.9 1.9 collective-permute-start.2
Sparse Core Ops, SparseCore 0:
  10.0 75.4 all-gather.5
  88.1 73.7 all-gather.7
  214.1 166.3 all-gather.9
where the time goes:
time: 437 us; the launch traced here: 434 us
  waiting for transfers between devices  256 us (59%)
  blocking collectives  52.3 us (12%)
  other arithmetic  49.5 us (11%)
  loops' own time  31.7 us (7%)
  local copies, waits for them, and re-layouts  16.8 us (4%)
  between operations  14.1 us (3%)
  starting transfers between devices  7.47 us (2%)
  matrix products  5.87 us (1%)
    all_gather x1, waiting for transfers between devices, prefix(): lax.all_gather(part.astype(kind), axis)  112 us
    all_gather x1, waiting for transfers between devices, on_device(): lax.all_gather(value_rows, 'ctx', axis=0, tiled=True)  76.4 us
    all_gather x1, waiting for transfers between devices, on_device(): lax.all_gather(key_rows, 'ctx', axis=0, tiled=True)  62.2 us
    all_gather x1, blocking collectives, prefix(): lax.all_gather(part.astype(kind), axis)  52.3 us
    select_n x32, other arithmetic, step(): return jax.tree.map(lambda a, b: jnp.where(reached, a, b), new, before)  41.4 us
    another operation x1, loops' own time, fold_keys(): lax.scan(visit, running, (jnp.arange(block_count, dtype=jnp.int32), key_b...  30.5 us
    dynamic_slice x16, local copies, waits for them, and re-layouts, fold_keys(): lax.scan(visit, running, (jnp.arange(block_count, dtype=jnp.int32), key_b...  10.2 us
  transfers between devices with their start and end apart: 6, of which 5 were waited for; matrix products, arithmetic and copies ran while one was open for 6% of the time, Pallas kernels for 0%

commit v1 on v0

v1 whole, which is shorter than its diff:
```python
import math

import jax
import jax.numpy as jnp
from jax import lax
from jax.experimental import pallas as pl
from jax.experimental.pallas import tpu as pltpu
from jax.sharding import PartitionSpec as P

EPSILON = 1e-05
NEGATIVE_FILL = -1e30
NEAR = 8
FAR = 4
SHARD = 128
ROW = NEAR * SHARD
CHUNK = 256
CHUNKS = ROW // CHUNK
HEAD = 128
STATE = 256
RIM = 16
PAST = 9 * CHUNK
QUERY_ROWS = SHARD + 16
PACK_ROWS = QUERY_ROWS + 2 * SHARD
EXP2_SCALE = math.log2(math.e) / math.sqrt(HEAD)
F32 = jnp.float32
BF16 = jnp.bfloat16


def near_groups():
    return [[x * NEAR + z for z in range(NEAR)] for x in range(FAR)]


def exchange_near(x):
    return lax.all_to_all(x, "ctx", 0, 0, axis_index_groups=near_groups(), tiled=True)


def from_row_behind(x, by):
    pairs = [(x0 * NEAR + z, (x0 + by) * NEAR + z) for x0 in range(FAR - by) for z in range(NEAR)]
    return lax.ppermute(x, "ctx", pairs)


def from_shard_behind(x):
    return lax.ppermute(x, "ctx", [(i, i + 1) for i in range(NEAR * FAR - 1)])


def with_partner(x):
    count = lax.axis_size("tp")
    return lax.ppermute(x, "tp", [(t, t ^ 1) for t in range(count)])


def first_tokens(docs, pos):
    begin = jnp.int32(0)
    first = pos
    for d in range(docs.shape[0]):
        first = jnp.where(pos >= begin, begin, first)
        begin = begin + docs[d]
    return first


def columns_of(rows):
    count = rows[0].shape[1]
    rows = list(rows) + [jnp.zeros((1, count), F32)] * (8 - len(rows))
    return jnp.transpose(jnp.concatenate(rows, 0))


def silu(v):
    return v / (1.0 + jnp.exp(-v))


def pair_kernel(keys, values, out):
    for n in range(NEAR):
        out[n, :, 0:HEAD] = keys[...]
        out[n, :, HEAD:] = values[...]


def pack_kernel(info, docs, queries, steps, raw, rim, taps, out, ext):
    ext[0:RIM] = rim[...].astype(F32)
    ext[RIM:] = raw[...].astype(F32)
    pos = info[3] + lax.broadcasted_iota(jnp.int32, (1, SHARD), 1)
    since = columns_of([(pos - first_tokens(docs, pos)).astype(F32)])[:, 0:1]
    acc = jnp.zeros((SHARD, STATE), F32)
    for m in range(4):
        part = ext[RIM - m : RIM - m + SHARD] * taps[3 - m : 4 - m]
        acc = acc + jnp.where(since >= m, part, 0.0)
    convolved = silu(acc).astype(BF16)
    wide = jnp.concatenate([steps[...], jnp.zeros((SHARD, HEAD - 2 * NEAR), F32)], 1)
    rows = jnp.transpose(wide)
    high = rows.astype(BF16).astype(F32)
    middle = (rows - high).astype(BF16).astype(F32)
    low = rows - high - middle
    for n in range(NEAR):
        out[n, 0:SHARD] = queries[:, n * HEAD : (n + 1) * HEAD]
        two = slice(2 * n, 2 * n + 2)
        out[n, SHARD:QUERY_ROWS] = jnp.concatenate(
            [high[two], middle[two], low[two], jnp.zeros((10, HEAD), F32)], 0
        ).astype(BF16)
        out[n, QUERY_ROWS : QUERY_ROWS + SHARD] = convolved[:, 0:HEAD]
        out[n, QUERY_ROWS + SHARD :] = convolved[:, HEAD:]


def two_heads(first, second, shape):
    lane = lax.broadcasted_iota(jnp.int32, shape, 1)
    return jnp.where(lane < HEAD // 2, jnp.broadcast_to(first, shape), jnp.broadcast_to(second, shape))


def mixing_kernel(
    info, docs, rates, received, other, mix, b_t, c_out, weigh, enter, enter_row, decays
):
    core_zero = info[2] == 0
    near = info[1]
    for s in range(NEAR):
        rows = slice(s * SHARD, (s + 1) * SHARD)
        for half in range(2):
            columns = slice(half * HEAD, (half + 1) * HEAD)
            at = slice(QUERY_ROWS + half * SHARD, QUERY_ROWS + (half + 1) * SHARD)
            from_other = slice(half * SHARD, (half + 1) * SHARD)
            mine, theirs = received[s, at], other[s, from_other]
            b_values = jnp.where(core_zero, mine, theirs)
            c_out[rows, columns] = jnp.where(core_zero, theirs, mine)
            b_t[columns, rows] = jnp.transpose(b_values.astype(F32)).astype(BF16)
    pieces = []
    for s in range(NEAR):
        piece = received[s, SHARD : SHARD + 16, :].astype(F32)
        pieces.append(piece[0:2] + piece[2:4] + piece[4:6])
    steps = jnp.concatenate(pieces, 1)
    rate = jnp.concatenate(
        [jnp.full((1, ROW), rates[2 * near], F32), jnp.full((1, ROW), rates[2 * near + 1], F32)], 0
    )
    log_decay = jnp.concatenate([-rate * steps, jnp.zeros((6, ROW), F32)], 0)
    row_start = info[0]
    pos = row_start + lax.broadcasted_iota(jnp.int32, (1, ROW), 1)
    first = first_tokens(docs, pos)
    below = lax.broadcasted_iota(jnp.int32, (CHUNK, CHUNK), 0)
    across = lax.broadcasted_iota(jnp.int32, (CHUNK, CHUNK), 1)
    upper = jnp.where(below <= across, 1.0, 0.0).astype(F32)
    before = jnp.zeros((2, 1), F32)
    decay_rows = []
    for k in range(CHUNKS):
        rows = slice(k * CHUNK, (k + 1) * CHUNK)
        chunk_start = row_start + k * CHUNK
        local = jnp.dot(
            log_decay[:, rows],
            upper,
            precision=lax.Precision.HIGHEST,
            preferred_element_type=F32,
        )[0:2]
        total = local[:, CHUNK - 1 : CHUNK]
        last_start = first[:, (k + 1) * CHUNK - 1 : (k + 1) * CHUNK]
        w = jnp.where(pos[:, rows] >= last_start, jnp.exp(total - local), 0.0) * steps[:, rows]
        e_chunk = jnp.where(first[:, rows] < chunk_start, jnp.exp(local), 0.0)
        e_row = jnp.where(first[:, rows] < row_start, jnp.exp(before + local), 0.0)
        crossing = jnp.where(last_start < chunk_start, jnp.exp(total), 0.0)
        decay_rows.append(two_heads(crossing[0:1], crossing[1:2], (1, HEAD)))
        before = before + total
        columns = jnp.transpose(jnp.concatenate([w, e_chunk, e_row, local], 0))
        since = columns_of([(first[:, rows] - chunk_start).astype(F32)])[:, 0:1]
        shape = (CHUNK, HEAD)
        weigh[rows] = two_heads(columns[:, 0:1], columns[:, 1:2], shape)
        enter[rows] = two_heads(columns[:, 2:3], columns[:, 3:4], shape)
        enter_row[rows] = two_heads(columns[:, 4:5], columns[:, 5:6], shape)
        gram = jnp.dot(c_out[rows], b_t[:, rows], preferred_element_type=F32)
        visible = (across <= below) & (across.astype(F32) >= since)
        for h in range(2):
            gap = jnp.where(visible, columns[:, 6 + h : 7 + h] - local[h : h + 1], NEGATIVE_FILL)
            mix[k, h] = (gram * jnp.exp(gap) * steps[h : h + 1, rows]).astype(BF16)
    last = jnp.where(first[:, ROW - 1 : ROW] < row_start, jnp.exp(before), 0.0)
    decay_rows.append(two_heads(last[0:1], last[1:2], (1, HEAD)))
    decays[...] = jnp.concatenate(decay_rows + [jnp.zeros((3, HEAD), F32)], 0)


def attend_kernel(
    info,
    docs,
    received,
    halo,
    own,
    back1,
    back2,
    back3,
    taps,
    b_t,
    weigh,
    decays,
    x_out,
    states,
    handed,
    keys,
    seen,
    top,
    total,
    summed,
    halo_seen,
    halo_top,
    halo_total,
    halo_summed,
    ext,
    sems,
):
    copies = [
        pltpu.make_async_copy(own, keys.at[pl.ds(PAST, ROW)], sems.at[0]),
        pltpu.make_async_copy(back1, keys.at[pl.ds(PAST - ROW, ROW)], sems.at[1]),
        pltpu.make_async_copy(back2, keys.at[pl.ds(PAST - 2 * ROW, ROW)], sems.at[2]),
        pltpu.make_async_copy(back3, keys.at[pl.ds(0, CHUNK)], sems.at[3]),
    ]
    for copy in copies:
        copy.start()
    row_start = info[0]
    near = info[1]
    pos = row_start + lax.broadcasted_iota(jnp.int32, (1, ROW), 1)
    first = first_tokens(docs, pos)
    columns = columns_of([(first - row_start).astype(F32), (pos - first).astype(F32)])
    since = columns[:, 1:2]
    seen[...] = jnp.broadcast_to(columns[:, 0:1], (ROW, HEAD))
    halo_pos = row_start - RIM + lax.broadcasted_iota(jnp.int32, (1, HEAD), 1)
    halo_first = columns_of([(first_tokens(docs, halo_pos) - row_start).astype(F32)])
    halo_seen[...] = jnp.broadcast_to(halo_first[0:RIM, 0:1], (RIM, HEAD))
    begin = jnp.int32(0)
    cross_start, cross_end = jnp.int32(0), jnp.int32(0)
    for d in range(docs.shape[0]):
        inside = begin <= row_start
        cross_start = jnp.where(inside, begin, cross_start)
        begin = begin + docs[d]
        cross_end = jnp.where(inside, begin, cross_end)
    lowest = lax.div(cross_start - row_start + PAST, jnp.int32(CHUNK))
    reached = cross_end - row_start

    def scores_of(query, block, seen_rows, causal):
        at = pl.ds(pl.multiple_of(block * CHUNK, CHUNK), CHUNK)
        raw = lax.dot_general(
            query, keys[at, 0:HEAD], (((1,), (1,)), ((), ())), preferred_element_type=F32
        )
        halves = []
        for half in range(2):
            offset = block * CHUNK - PAST + half * HEAD
            place = lax.broadcasted_iota(jnp.int32, (1, HEAD), 1) + offset
            visible = place.astype(F32) >= seen_rows
            if causal is not None:
                down = lax.broadcasted_iota(jnp.int32, (query.shape[0], HEAD), 0) + causal
                along = lax.broadcasted_iota(jnp.int32, (query.shape[0], HEAD), 1) + half * HEAD
                visible = visible & (along <= down)
            part = raw[:, half * HEAD : (half + 1) * HEAD]
            halves.append(jnp.where(visible, part, NEGATIVE_FILL))
        return halves, keys[at, HEAD:]

    def fold(query, block, seen_ref, top_ref, total_ref, summed_ref, rows, causal, fresh):
        (left, right), values = scores_of(query, block, seen_ref[rows], causal)
        largest = jnp.max(jnp.maximum(left, right), axis=1, keepdims=True)
        if fresh:
            new_top = jnp.broadcast_to(largest, left.shape)
        else:
            old_top = top_ref[rows]
            new_top = jnp.maximum(old_top, largest)
            factor = jnp.exp2((old_top - new_top) * EXP2_SCALE)
        left = jnp.exp2((left - new_top) * EXP2_SCALE)
        right = jnp.exp2((right - new_top) * EXP2_SCALE)
        weights = jnp.concatenate([left.astype(BF16), right.astype(BF16)], 1)
        product = jnp.dot(weights, values, preferred_element_type=F32)
        top_ref[rows] = new_top
        if fresh:
            total_ref[rows] = left + right
            summed_ref[rows] = product
        else:
            total_ref[rows] = total_ref[rows] * factor + (left + right)
            summed_ref[rows] = summed_ref[rows] * factor + product

    def query_of(i):
        return received[2 * i : 2 * i + 2, 0:SHARD, :].reshape(CHUNK, HEAD)

    def fold_row(i, block, causal, fresh):
        fold(
            query_of(i),
            block,
            seen,
            top,
            total,
            summed,
            slice(i * CHUNK, (i + 1) * CHUNK),
            causal,
            fresh,
        )

    def fold_halo(block, causal, fresh):
        fold(
            halo[...],
            block,
            halo_seen,
            halo_top,
            halo_total,
            halo_summed,
            slice(0, RIM),
            causal,
            fresh,
        )

    for copy in copies:
        copy.wait()
    own_block = PAST // CHUNK
    fold_halo(own_block - 1, CHUNK - RIM, True)
    for back in range(CHUNKS):
        for i in range(back, CHUNKS):
            fold_row(i, own_block + i - back, 0 if back == 0 else None, back == 0)

    def earlier(count):
        def visit(n, carry):
            block = own_block - 1 - n
            for i in range(count):
                fold_row(i, block, None, False)

            @pl.when(n > 0)
            def _():
                fold_halo(block, None, False)

            return carry

        lax.fori_loop(0, own_block - lowest, visit, 0)

    @pl.when(reached <= CHUNK)
    def _():
        earlier(1)

    @pl.when((reached > CHUNK) & (reached <= 2 * CHUNK))
    def _():
        earlier(2)

    @pl.when(reached > 2 * CHUNK)
    def _():
        earlier(CHUNKS)

    def finish(total_ref, summed_ref):
        whole = jnp.sum(total_ref[...], axis=1, keepdims=True)
        return (summed_ref[...] / whole).astype(BF16).astype(F32)

    ext[0:RIM] = finish(halo_total, halo_summed)
    ext[RIM:] = finish(total, summed)
    own_taps = taps[:, pl.ds(pl.multiple_of(near * HEAD, HEAD), HEAD)]
    state = jnp.zeros((STATE, HEAD), F32)
    for k in range(CHUNKS):
        rows = slice(k * CHUNK, (k + 1) * CHUNK)
        acc = jnp.zeros((CHUNK, HEAD), F32)
        for m in range(4):
            part = ext[RIM - m + k * CHUNK : RIM - m + (k + 1) * CHUNK] * own_taps[3 - m : 4 - m]
            acc = acc + jnp.where(since[rows] >= m, part, 0.0)
        x = silu(acc).astype(BF16)
        x_out[rows] = x
        states[k] = state.astype(BF16)
        weighed = (x.astype(F32) * weigh[rows]).astype(BF16)
        state = state * decays[k : k + 1] + jnp.dot(
            b_t[:, rows], weighed, preferred_element_type=F32
        )
    handed[0:STATE] = state.astype(BF16)
    decay = decays[CHUNKS : CHUNKS + 1]
    high = decay.astype(BF16).astype(F32)
    handed[STATE:] = jnp.concatenate(
        [high, decay - high, jnp.zeros((14, HEAD), F32)], 0
    ).astype(BF16)


def inner_kernel(info, skip, mix, x_in, c_in, states, enter, y_out):
    near = info[1]
    gain = two_heads(skip[2 * near], skip[2 * near + 1], (1, HEAD))
    lane = lax.broadcasted_iota(jnp.int32, (CHUNK, HEAD), 1)
    for k in range(CHUNKS):
        rows = slice(k * CHUNK, (k + 1) * CHUNK)
        x = x_in[rows]
        left = jnp.dot(mix[k, 0], x, preferred_element_type=F32)
        right = jnp.dot(mix[k, 1], x, preferred_element_type=F32)
        y = jnp.where(lane < HEAD // 2, left, right) + x.astype(F32) * gain
        if k > 0:
            y = y + enter[rows] * jnp.dot(c_in[rows], states[k], preferred_element_type=F32)
        y_out[rows] = y


def carried_kernel(y_in, enter_row, c_in, back1, back2, back3, y_out):
    def parts(ref):
        tail = ref[STATE:].astype(F32)
        return ref[0:STATE].astype(F32), tail[0:1] + tail[1:2]

    state1, decay1 = parts(back1)
    state2, decay2 = parts(back2)
    state3, _ = parts(back3)
    entering = (state1 + decay1 * (state2 + decay2 * state3)).astype(BF16)
    for k in range(CHUNKS):
        rows = slice(k * CHUNK, (k + 1) * CHUNK)
        carried = jnp.dot(c_in[rows], entering, preferred_element_type=F32)
        y_out[rows] = (y_in[rows] + enter_row[rows] * carried).astype(BF16)


def gated_of(y, gate, h):
    return y[h].astype(F32) * silu(gate[:, h * HEAD : (h + 1) * HEAD].astype(F32))


def square_kernel(y, gate, sums):
    acc = jnp.zeros((SHARD, HEAD), F32)
    for h in range(NEAR):
        gated = gated_of(y, gate, h)
        acc = acc + gated * gated
    sums[...] = jnp.broadcast_to(jnp.sum(acc, axis=1, keepdims=True), (SHARD, HEAD))


def norm_kernel(y, gate, sums, partner, gain, out):
    mean = (sums[...] + partner[...]) / (2.0 * NEAR * HEAD)
    scale = lax.rsqrt(mean + EPSILON)
    for h in range(NEAR):
        columns = slice(h * HEAD, (h + 1) * HEAD)
        out[:, columns] = (gated_of(y, gate, h) * scale * gain[:, columns]).astype(BF16)


def call(kernel, outs, args, smem=0, raw=(), scratch=(), flops=0, mib=48):
    specs = []
    for n in range(len(args)):
        if n < smem:
            specs.append(pl.BlockSpec(memory_space=pltpu.SMEM))
        elif n in raw:
            specs.append(pl.BlockSpec(memory_space=pl.ANY))
        else:
            specs.append(pl.BlockSpec(memory_space=pltpu.VMEM))
    single = len(outs) == 1
    shapes = [jax.ShapeDtypeStruct(shape, kind) for shape, kind in outs]
    out_specs = [pl.BlockSpec(memory_space=pltpu.VMEM)] * len(outs)
    return pl.pallas_call(
        kernel,
        out_shape=shapes[0] if single else shapes,
        in_specs=specs,
        out_specs=out_specs[0] if single else out_specs,
        scratch_shapes=list(scratch),
        compiler_params=pltpu.CompilerParams(vmem_limit_bytes=mib * 1024 * 1024),
        cost_estimate=pl.CostEstimate(flops=flops, bytes_accessed=1 << 21, transcendentals=0),
    )(*args)


def on_device(
    queries,
    key_rows,
    value_rows,
    doc_lengths,
    gate_input,
    bc_input,
    step_size,
    decay_rate,
    skip_gain,
    conv_x,
    conv_bc,
    norm_gain,
):
    ctx = lax.axis_index("ctx")
    tp = lax.axis_index("tp")
    near = ctx % NEAR
    core = tp % 2
    group = tp // 2
    info = jnp.stack([(ctx // NEAR) * ROW, near, core, ctx * SHARD]).astype(jnp.int32)

    own = exchange_near(
        call(pair_kernel, [((NEAR, SHARD, 2 * HEAD), BF16)], (key_rows, value_rows)).reshape(
            ROW, 2 * HEAD
        )
    )
    bc_mine = lax.dynamic_slice(bc_input, (0, core, group, 0), (SHARD, 1, 1, STATE)).reshape(
        SHARD, STATE
    )
    taps_mine = lax.dynamic_slice(conv_bc, (0, core, group, 0), (4, 1, 1, STATE)).reshape(4, STATE)
    rim = from_shard_behind(bc_mine[SHARD - RIM :])
    packed = call(
        pack_kernel,
        [((NEAR, PACK_ROWS, HEAD), BF16)],
        (info, doc_lengths, queries, step_size, bc_mine, rim, taps_mine),
        smem=2,
        scratch=[pltpu.VMEM((RIM + SHARD, STATE), F32)],
    )
    back1 = from_row_behind(own, 1)
    back2 = from_row_behind(own, 2)
    back3 = from_row_behind(own[ROW - CHUNK :], 3)
    received = exchange_near(packed.reshape(NEAR * PACK_ROWS, HEAD)).reshape(
        NEAR, PACK_ROWS, HEAD
    )
    halo = from_row_behind(received[NEAR - 1, SHARD - RIM : SHARD], 1)
    other = with_partner(received[:, QUERY_ROWS:])
    mix, b_t, c_row, weigh, enter, enter_row, decays = call(
        mixing_kernel,
        [
            ((CHUNKS, 2, CHUNK, CHUNK), BF16),
            ((STATE, ROW), BF16),
            ((ROW, STATE), BF16),
            ((ROW, HEAD), F32),
            ((ROW, HEAD), F32),
            ((ROW, HEAD), F32),
            ((8, HEAD), F32),
        ],
        (info, doc_lengths, decay_rate, received, other),
        smem=3,
        flops=1 << 28,
    )
    x, states, handed = call(
        attend_kernel,
        [
            ((ROW, HEAD), BF16),
            ((CHUNKS, STATE, HEAD), BF16),
            ((STATE + 16, HEAD), BF16),
        ],
        (info, doc_lengths, received, halo, own, back1, back2, back3, conv_x, b_t, weigh, decays),
        smem=2,
        raw=(4, 5, 6, 7),
        scratch=[
            pltpu.VMEM((PAST + ROW, 2 * HEAD), BF16),
            pltpu.VMEM((ROW, HEAD), F32),
            pltpu.VMEM((ROW, HEAD), F32),
            pltpu.VMEM((ROW, HEAD), F32),
            pltpu.VMEM((ROW, HEAD), F32),
            pltpu.VMEM((RIM, HEAD), F32),
            pltpu.VMEM((RIM, HEAD), F32),
            pltpu.VMEM((RIM, HEAD), F32),
            pltpu.VMEM((RIM, HEAD), F32),
            pltpu.VMEM((RIM + ROW, HEAD), F32),
            pltpu.SemaphoreType.DMA((4,)),
        ],
        flops=1 << 30,
    )
    handed1 = from_row_behind(handed, 1)
    handed2 = from_row_behind(handed, 2)
    handed3 = from_row_behind(handed, 3)
    y_inner = call(
        inner_kernel,
        [((ROW, HEAD), F32)],
        (info, skip_gain, mix, x, c_row, states, enter),
        smem=2,
        flops=1 << 28,
    )
    y_row = call(
        carried_kernel,
        [((ROW, HEAD), BF16)],
        (y_inner, enter_row, c_row, handed1, handed2, handed3),
    )
    y_heads = exchange_near(y_row).reshape(NEAR, SHARD, HEAD)
    sums = call(square_kernel, [((SHARD, HEAD), F32)], (y_heads, gate_input))
    partner = with_partner(sums)
    return call(
        norm_kernel,
        [((SHARD, NEAR * HEAD), BF16)],
        (y_heads, gate_input, sums, partner, norm_gain.reshape(1, -1)),
    )


def solution(mesh):
    return jax.shard_map(
        on_device,
        mesh=mesh,
        in_specs=(
            P("ctx", "tp"),
            P("ctx", "tp"),
            P("ctx", "tp"),
            P(),
            P("ctx", "tp"),
            P("ctx", None, None, None),
            P("ctx", "tp"),
            P("tp"),
            P("tp"),
            P(None, "tp"),
            P(),
            P("tp"),
        ),
        out_specs=P("ctx", "tp"),
        check_vma=False,
    )
```

time: 437 us -> 126 us (0.29)
  waiting for transfers between devices: 256 us -> 47 us
  other arithmetic: 49.5 us -> 0.08 us
  starting transfers between devices: 7.47 us -> 47.6 us
  blocking collectives: 52.3 us -> 12.7 us
  loops' own time: 31.7 us -> 0 us
  between operations: 14.1 us -> 0.3 us
  Pallas kernels: 0 us -> 12.9 us
  local copies, waits for them, and re-layouts: 16.8 us -> 4.1 us
  matrix products: 5.87 us -> 0 us
    all_gather x3 -> x0, waiting for transfers between devices: 251 us -> none  [the longest x1 112 us: prefix(): lax.all_gather(part.astype(kind), axis)]
    all_gather x1 -> x0, blocking collectives: 52.3 us -> none  [prefix(): lax.all_gather(part.astype(kind), axis)]
    select_n x32 -> x0, other arithmetic: 41.4 us -> none  [step(): return jax.tree.map(lambda a, b: jnp.where(reached, a, b), new, before)]
    all_to_all x0 -> x2, waiting for transfers between devices: none -> 35 us  [exchange_near(): lax.all_to_all(x, 'ctx', 0, 0, axis_index_groups=near_groups(), tiled=True)]
    another operation x18 -> x0, loops' own time: 31.7 us -> none  [the longest x1 30.5 us: fold_keys(): lax.scan(visit, running, (jnp.arange(block_count, dtype=jnp.int32), key_b...]
    ppermute x3 -> x10, starting transfers between devices: 7.39 us -> 35.4 us  [the longest x7 26 us: from_row_behind(): return lax.ppermute(x, 'ctx', pairs)]
    pallas_call x0 -> x8, Pallas kernels: none -> 12.9 us  [call(): pl.pallas_call(kernel, out_shape=shapes[0] if single else shapes, in_spec...]
    all_to_all x0 -> x1, blocking collectives: none -> 12.7 us  [exchange_near(): lax.all_to_all(x, 'ctx', 0, 0, axis_index_groups=near_groups(), tiled=True)]
  transfers between devices with their start and end apart: 6 -> 12, of which waited for: 5 -> 6; matrix products, arithmetic and copies ran while one was open for 6% -> 1% of each run, Pallas kernels for 0% -> 5%
where the time goes in v1:
time: 126 us; the launch traced here: 125 us
  starting transfers between devices  47.6 us (38%)
  waiting for transfers between devices  47 us (37%)
  Pallas kernels  12.9 us (10%)
  blocking collectives  12.7 us (10%)
  local copies, waits for them, and re-layouts  4.1 us (3%)
    all_to_all x2, waiting for transfers between devices, exchange_near(): lax.all_to_all(x, 'ctx', 0, 0, axis_index_groups=near_groups(), tiled=True)  35 us
    ppermute x7, starting transfers between devices, from_row_behind(): return lax.ppermute(x, 'ctx', pairs)  26 us
    pallas_call x8, Pallas kernels, call(): pl.pallas_call(kernel, out_shape=shapes[0] if single else shapes, in_spec...  12.9 us
    all_to_all x1, blocking collectives, exchange_near(): lax.all_to_all(x, 'ctx', 0, 0, axis_index_groups=near_groups(), tiled=True)  12.7 us
    all_to_all x2, starting transfers between devices, exchange_near(): lax.all_to_all(x, 'ctx', 0, 0, axis_index_groups=near_groups(), tiled=True)  12.2 us
    ppermute x7, waiting for transfers between devices, from_row_behind(): return lax.ppermute(x, 'ctx', pairs)  11.1 us
    ppermute x2, starting transfers between devices, with_partner(): return lax.ppermute(x, 'tp', [(t, t ^ 1) for t in range(count)])  4.91 us
    ppermute x1, starting transfers between devices, from_shard_behind(): return lax.ppermute(x, 'ctx', [(i, i + 1) for i in range(NEAR * FAR - 1)])  4.5 us
  transfers between devices with their start and end apart: 12, of which 6 were waited for; matrix products, arithmetic and copies ran while one was open for 1% of the time, Pallas kernels for 5%

profile of v1, /device:TPU:1, one launch (start us, length us, event | category | flops | bytes accessed | tf_op | source)
XLA Modules:
  0.0 124.7 jit_solution(8257184565560804534)
XLA Ops:
  0.0 0.0 copy-start
  0.0 1.0 copy-done
  1.0 0.1 constant_dynamic-slice_fusion.1
  1.2 0.0 copy-start.2
  1.2 4.5 %collective-permute-start = (bf16[16,256]{1,0:T(8,128)(2,1)S(1)}, bf16[16,256]{1,0:T(8,128)(2,1)S(1)}, u32[]{:S(2)}, u32[]{:S(2)}) collective-permute-start(bf16[16,256]{1,0:T(8,128)(2,1)S(1)} %slice_bitcast_fusion), channel_id=1, source_target_pairs={{0,8},{8,16},{16,24},{24,32},{32,40},{40,48},{48,56},{56,64},{64,7... | collective-permute-start | bytes 24584 | tf_op jit(solution)/shard_map/ppermute | solution.py:43
  5.8 0.7 constant_dynamic-slice_fusion
  6.5 0.1 pad_add_fusion.info
  6.6 0.0 copy-start.10
  6.6 0.7 copy-done.10
  7.3 0.1 copy.16.steps
  7.4 0.0 collective-permute-done.rim
  7.4 0.0 copy-start.6
  7.4 0.0 copy-done.2
  7.4 0.6 copy-done.6
  8.0 1.7 %shard_map.118 = bf16[8,400,128]{2,1,0:T(8,128)(2,1)} custom-call(s32[4]{0:T(128)S(1)} %pad_add_fusion.info, s32[16]{0:T(128)S(1)} %copy-done.6, bf16[128,1024]{1,0:T(8,128)(2,1)S(1)} %copy-done.2, f32[128,16]{1,0:T(8,128)S(1)} %copy.16.steps, bf16[128,256]{1,0:T(8,128)(2,1)S(1)} %bitcast.22, bf16[16,256]{1,0:T(8,128)(2,1)S(1)} %collective-permute-done.rim, ...), custom_call_target="tpu_custom_call" | custom-call | bytes 2097152 | tf_op jit(solution)/shard_map/pallas_call | solution.py:420
  9.8 0.0 copy-start.3
  9.8 0.0 copy-start.4
  9.8 8.7 %all-to-all-start = ((bf16[8,400,128]{2,1,0:T(8,128)(2,1)}), bf16[8,400,128]{2,1,0:T(8,128)(2,1)S(1)}, u32[]{:S(2)}, u32[]{:S(2)}) async-start(bf16[8,400,128]{2,1,0:T(8,128)(2,1)} %shard_map.118), calls=%async_computation | async-start | bytes 1638400 | tf_op jit(solution)/shard_map/all_to_all | solution.py:34
  18.5 0.0 copy-done.3
  18.5 0.0 copy-done.4
  18.5 0.9 shard_map.120
  19.4 21.7 %all-to-all-done.received = bf16[8,400,128]{2,1,0:T(8,128)(2,1)S(1)} async-done(((bf16[8,400,128]{2,1,0:T(8,128)(2,1)}), bf16[8,400,128]{2,1,0:T(8,128)(2,1)S(1)}, u32[]{:S(2)}, u32[]{:S(2)}) %all-to-all-start) | async-done | bytes 819232 | tf_op jit(solution)/shard_map/all_to_all | solution.py:34
  41.2 3.5 %all-to-all-start.1 = ((bf16[8,128,256]{2,1,0:T(8,128)(2,1)}), bf16[8,128,256]{2,1,0:T(8,128)(2,1)S(1)}, u32[]{:S(2)}, u32[]{:S(2)}) async-start(bf16[8,128,256]{2,1,0:T(8,128)(2,1)} %shard_map.120), calls=%async_computation.1 | async-start | bytes 1048576 | tf_op jit(solution)/shard_map/all_to_all | solution.py:34
  44.7 2.2 %collective-permute-start.1 = (bf16[8,256,128]{2,1,0:T(8,128)(2,1)S(1)}, bf16[8,256,128]{2,1,0:T(8,128)(2,1)S(1)}, u32[]{:S(2)}, u32[]{:S(2)}) collective-permute-start(bf16[8,256,128]{2,1,0:T(8,128)(2,1)S(1)} %slice.25), channel_id=1, source_target_pairs={{0,1},{1,0},{2,3},{3,2},{4,5},{5,4},{6,7},{7,6},{8,9},{9,8},{10,11... | collective-permute-start | bytes 1572872 | tf_op jit(solution)/shard_map/ppermute | solution.py:48
  46.9 13.2 %all-to-all-done.1 = bf16[8,128,256]{2,1,0:T(8,128)(2,1)S(1)} async-done(((bf16[8,128,256]{2,1,0:T(8,128)(2,1)}), bf16[8,128,256]{2,1,0:T(8,128)(2,1)S(1)}, u32[]{:S(2)}, u32[]{:S(2)}) %all-to-all-start.1) | async-done | bytes 524320 | tf_op jit(solution)/shard_map/all_to_all | solution.py:34
  60.2 4.7 %collective-permute-start.4 = (bf16[1024,256]{1,0:T(8,128)(2,1)S(1)}, bf16[1024,256]{1,0:T(8,128)(2,1)S(1)}, u32[]{:S(2)}, u32[]{:S(2)}) collective-permute-start(bf16[1024,256]{1,0:T(8,128)(2,1)S(1)} %bitcast.19), channel_id=1, source_target_pairs={{0,128},{8,136},{16,144},{24,152},{32,160},{40,168},{48,176},{56,1... | collective-permute-start | bytes 1572872 | tf_op jit(solution)/shard_map/ppermute | solution.py:39
  64.8 2.2 %collective-permute-start.3 = (bf16[1024,256]{1,0:T(8,128)(2,1)S(1)}, bf16[1024,256]{1,0:T(8,128)(2,1)S(1)}, u32[]{:S(2)}, u32[]{:S(2)}) collective-permute-start(bf16[1024,256]{1,0:T(8,128)(2,1)S(1)} %bitcast.20), channel_id=1, source_target_pairs={{0,64},{8,72},{16,80},{24,88},{32,96},{40,104},{48,112},{56,120},{... | collective-permute-start | bytes 1572872 | tf_op jit(solution)/shard_map/ppermute | solution.py:39
  67.1 0.0 copy-start.7
  67.1 1.3 %collective-permute-start.5 = (bf16[256,256]{1,0:T(8,128)(2,1)S(1)}, bf16[256,256]{1,0:T(8,128)(2,1)S(1)}, u32[]{:S(2)}, u32[]{:S(2)}) collective-permute-start(bf16[256,256]{1,0:T(8,128)(2,1)S(1)} %bitcast.25), channel_id=1, source_target_pairs={{0,192},{8,200},{16,208},{24,216},{32,224},{40,232},{48,240},{56,2... | collective-permute-start | bytes 393224 | tf_op jit(solution)/shard_map/ppermute | solution.py:39
  68.4 0.0 copy-start.9
  68.5 1.3 %collective-permute-start.2 = (bf16[16,128]{1,0:T(8,128)(2,1)S(1)}, bf16[16,128]{1,0:T(8,128)(2,1)S(1)}, u32[]{:S(2)}, u32[]{:S(2)}) collective-permute-start(bf16[16,128]{1,0:T(8,128)(2,1)S(1)} %slice_bitcast_fusion.1), channel_id=1, source_target_pairs={{0,64},{8,72},{16,80},{24,88},{32,96},{40,104},{48,112},{56,120},{... | collective-permute-start | bytes 12296 | tf_op jit(solution)/shard_map/ppermute | solution.py:39
  69.8 0.0 collective-permute-done.1.other
  69.8 0.0 copy-done.7
  69.8 3.7 %shard_map.119 = (bf16[4,2,256,256]{3,2,1,0:T(8,128)(2,1)S(1)}, bf16[256,1024]{1,0:T(8,128)(2,1)S(1)}, bf16[1024,256]{1,0:T(8,128)(2,1)S(1)}, f32[1024,128]{1,0:...) custom-call(s32[4]{0:T(128)S(1)} %pad_add_fusion.info, s32[16]{0:T(128)S(1)} %copy-done.6, ...), custom_call_target="tpu_custom_call" | custom-call | flops 268435456 | bytes 2097152 | tf_op jit(solution)/shard_map/pallas_call | solution.py:420
  73.4 5.8 %collective-permute-done.5.back3 = bf16[256,256]{1,0:T(8,128)(2,1)S(1)} collective-permute-done((bf16[256,256]{1,0:T(8,128)(2,1)S(1)}, bf16[256,256]{1,0:T(8,128)(2,1)S(1)}, u32[]{:S(2)}, u32[]{:S(2)}) %collective-permute-start.5) | collective-permute-done | bytes 131104 | tf_op jit(solution)/shard_map/ppermute | solution.py:39
  79.3 0.0 collective-permute-done.4.back2
  79.3 5.2 %collective-permute-done.3.back1 = bf16[1024,256]{1,0:T(8,128)(2,1)S(1)} collective-permute-done((bf16[1024,256]{1,0:T(8,128)(2,1)S(1)}, bf16[1024,256]{1,0:T(8,128)(2,1)S(1)}, u32[]{:S(2)}, u32[]{:S(2)}) %collective-permute-start.3) | collective-permute-done | bytes 524320 | tf_op jit(solution)/shard_map/ppermute | solution.py:39
  84.5 0.1 collective-permute-done.2.halo
  84.6 0.0 copy-done.9
  84.6 4.0 %shard_map.121 = (bf16[1024,128]{1,0:T(8,128)(2,1)S(1)}, bf16[4,256,128]{2,1,0:T(8,128)(2,1)S(1)}, bf16[272,128]{1,0:T(8,128)(2,1)S(1)}) custom-call(s32[4]{0:T(128)S(1)} %pad_add_fusion.info, s32[16]{0:T(128)S(1)} %copy-done.6, bf16[8,400,128]{2,1,0:T(8,128)(2,1)S(1)} %all-to-all-done.received, bf16[16,128]{1,0:T(8,128)(2,1)S(1)} %collective-permute-done.2.halo, ...), custom_call_target="tpu_custom_call" | custom-call | flops 1073741824 | bytes 2097152 | tf_op jit(solution)/shard_map/pallas_call | solution.py:420
  88.6 1.3 %collective-permute-start.8 = (bf16[272,128]{1,0:T(8,128)(2,1)S(1)}, bf16[272,128]{1,0:T(8,128)(2,1)S(1)}, u32[]{:S(2)}, u32[]{:S(2)}) collective-permute-start(bf16[272,128]{1,0:T(8,128)(2,1)S(1)} %get-tuple-element.24), channel_id=1, source_target_pairs={{0,192},{8,200},{16,208},{24,216},{32,224},{40,232},{48,240},{56,2... | collective-permute-start | bytes 208904 | tf_op jit(solution)/shard_map/ppermute | solution.py:39
  89.9 13.9 %collective-permute-start.7 = (bf16[272,128]{1,0:T(8,128)(2,1)S(1)}, bf16[272,128]{1,0:T(8,128)(2,1)S(1)}, u32[]{:S(2)}, u32[]{:S(2)}) collective-permute-start(bf16[272,128]{1,0:T(8,128)(2,1)S(1)} %get-tuple-element.24), channel_id=1, source_target_pairs={{0,128},{8,136},{16,144},{24,152},{32,160},{40,168},{48,176},{56,1... | collective-permute-start | bytes 208904 | tf_op jit(solution)/shard_map/ppermute | solution.py:39
  103.8 1.3 %collective-permute-start.6 = (bf16[272,128]{1,0:T(8,128)(2,1)S(1)}, bf16[272,128]{1,0:T(8,128)(2,1)S(1)}, u32[]{:S(2)}, u32[]{:S(2)}) collective-permute-start(bf16[272,128]{1,0:T(8,128)(2,1)S(1)} %get-tuple-element.24), channel_id=1, source_target_pairs={{0,64},{8,72},{16,80},{24,88},{32,96},{40,104},{48,112},{56,120},{... | collective-permute-start | bytes 208904 | tf_op jit(solution)/shard_map/ppermute | solution.py:39
  105.1 0.0 copy-start.8
  105.1 0.6 copy-done.8
  105.7 1.1 shard_map.122.y_in
  106.8 0.0 collective-permute-done.8.back3
  106.8 0.0 collective-permute-done.7.back2
  106.8 0.0 collective-permute-done.6.back1
  106.8 0.3 shard_map.123
  107.1 0.0 copy-start.1
  107.2 12.7 %all_to_all.23.y = bf16[8,128,128]{2,1,0:T(8,128)(2,1)S(1)} all-to-all(bf16[8,128,128]{2,1,0:T(8,128)(2,1)S(1)} %bitcast.18), channel_id=1, replica_groups={{0,8,16,24,32,40,48,56},{64,72,80,88,96,104,112,120},{128,136,144,152,1..., dimensions={0} | all-to-all | bytes 524288 | tf_op jit(solution)/shard_map/all_to_all | solution.py:34
  119.9 0.0 copy-done.1
  119.9 0.0 copy-start.5
  119.9 0.3 shard_map.124.sums
  120.1 2.7 %collective-permute-start.9 = (f32[128,128]{1,0:T(8,128)S(1)}, f32[128,128]{1,0:T(8,128)S(1)}, u32[]{:S(2)}, u32[]{:S(2)}) collective-permute-start(f32[128,128]{1,0:T(8,128)S(1)} %shard_map.124.sums), channel_id=1, source_target_pairs={{0,1},{1,0},{2,3},{3,2},{4,5},{5,4},{6,7},{7,6},{8,9},{9,8},{10,11... | collective-permute-start | bytes 196616 | tf_op jit(solution)/shard_map/ppermute | solution.py:48
  122.8 0.9 collective-permute-done.9.partner
  123.7 0.0 copy-done.5
  123.7 0.9 shard_map.125
  (7 shorter events, 0.1 us)
Async XLA Ops:
  0.0 1.0 copy-start
  1.2 6.2 %copy-start.2 = (bf16[128,1024]{1,0:T(8,128)(2,1)S(1)}, bf16[128,1024]{1,0:T(8,128)(2,1)}, u32[]{:S(2)}) copy-start(bf16[128,1024]{1,0:T(8,128)(2,1)} %queries.1) | copy-start | bytes 786436
  1.2 6.2 %collective-permute-start = (bf16[16,256]{1,0:T(8,128)(2,1)S(1)}, bf16[16,256]{1,0:T(8,128)(2,1)S(1)}, u32[]{:S(2)}, u32[]{:S(2)}) collective-permute-start(bf16[16,256]{1,0:T(8,128)(2,1)S(1)} %slice_bitcast_fusion), channel_id=1, source_target_pairs={{0,8},{8,16},{16,24},{24,32},{32,40},{40,48},{48,56},{56,64},{64,7... | collective-permute-start | bytes 24584 | tf_op jit(solution)/shard_map/ppermute | solution.py:43
  6.6 0.7 copy-start.10
  7.4 0.7 copy-start.6
  9.8 8.7 %copy-start.3 = (bf16[128,128]{1,0:T(8,128)(2,1)S(1)}, bf16[128,128]{1,0:T(8,128)(2,1)}, u32[]{:S(2)}) copy-start(bf16[128,128]{1,0:T(8,128)(2,1)} %keys.1) | copy-start | bytes 98308
  9.8 8.7 %copy-start.4 = (bf16[128,128]{1,0:T(8,128)(2,1)S(1)}, bf16[128,128]{1,0:T(8,128)(2,1)}, u32[]{:S(2)}) copy-start(bf16[128,128]{1,0:T(8,128)(2,1)} %values.1) | copy-start | bytes 98308
  9.8 31.4 %all-to-all-start = ((bf16[8,400,128]{2,1,0:T(8,128)(2,1)}), bf16[8,400,128]{2,1,0:T(8,128)(2,1)S(1)}, u32[]{:S(2)}, u32[]{:S(2)}) async-start(bf16[8,400,128]{2,1,0:T(8,128)(2,1)} %shard_map.118), calls=%async_computation | async-start | bytes 1638400 | tf_op jit(solution)/shard_map/all_to_all | solution.py:34
  41.2 19.0 %all-to-all-start.1 = ((bf16[8,128,256]{2,1,0:T(8,128)(2,1)}), bf16[8,128,256]{2,1,0:T(8,128)(2,1)S(1)}, u32[]{:S(2)}, u32[]{:S(2)}) async-start(bf16[8,128,256]{2,1,0:T(8,128)(2,1)} %shard_map.120), calls=%async_computation.1 | async-start | bytes 1048576 | tf_op jit(solution)/shard_map/all_to_all | solution.py:34
  44.7 25.1 %collective-permute-start.1 = (bf16[8,256,128]{2,1,0:T(8,128)(2,1)S(1)}, bf16[8,256,128]{2,1,0:T(8,128)(2,1)S(1)}, u32[]{:S(2)}, u32[]{:S(2)}) collective-permute-start(bf16[8,256,128]{2,1,0:T(8,128)(2,1)S(1)} %slice.25), channel_id=1, source_target_pairs={{0,1},{1,0},{2,3},{3,2},{4,5},{5,4},{6,7},{7,6},{8,9},{9,8},{10,11... | collective-permute-start | bytes 1572872 | tf_op jit(solution)/shard_map/ppermute | solution.py:48
  60.2 19.1 %collective-permute-start.4 = (bf16[1024,256]{1,0:T(8,128)(2,1)S(1)}, bf16[1024,256]{1,0:T(8,128)(2,1)S(1)}, u32[]{:S(2)}, u32[]{:S(2)}) collective-permute-start(bf16[1024,256]{1,0:T(8,128)(2,1)S(1)} %bitcast.19), channel_id=1, source_target_pairs={{0,128},{8,136},{16,144},{24,152},{32,160},{40,168},{48,176},{56,1... | collective-permute-start | bytes 1572872 | tf_op jit(solution)/shard_map/ppermute | solution.py:39
  64.8 19.6 %collective-permute-start.3 = (bf16[1024,256]{1,0:T(8,128)(2,1)S(1)}, bf16[1024,256]{1,0:T(8,128)(2,1)S(1)}, u32[]{:S(2)}, u32[]{:S(2)}) collective-permute-start(bf16[1024,256]{1,0:T(8,128)(2,1)S(1)} %bitcast.20), channel_id=1, source_target_pairs={{0,64},{8,72},{16,80},{24,88},{32,96},{40,104},{48,112},{56,120},{... | collective-permute-start | bytes 1572872 | tf_op jit(solution)/shard_map/ppermute | solution.py:39
  67.1 2.7 %copy-start.7 = (f32[16]{0:T(128)S(1)}, f32[16]{0:T(128)}, u32[]{:S(2)}) copy-start(f32[16]{0:T(128)} %rates.1) | copy-start | bytes 196
  67.1 12.1 %collective-permute-start.5 = (bf16[256,256]{1,0:T(8,128)(2,1)S(1)}, bf16[256,256]{1,0:T(8,128)(2,1)S(1)}, u32[]{:S(2)}, u32[]{:S(2)}) collective-permute-start(bf16[256,256]{1,0:T(8,128)(2,1)S(1)} %bitcast.25), channel_id=1, source_target_pairs={{0,192},{8,200},{16,208},{24,216},{32,224},{40,232},{48,240},{56,2... | collective-permute-start | bytes 393224 | tf_op jit(solution)/shard_map/ppermute | solution.py:39
  68.4 16.1 %copy-start.9 = (f32[4,1024]{1,0:T(4,128)S(1)}, f32[4,1024]{1,0:T(4,128)}, u32[]{:S(2)}) copy-start(f32[4,1024]{1,0:T(4,128)} %taps.1) | copy-start | bytes 49156
  68.5 16.1 %collective-permute-start.2 = (bf16[16,128]{1,0:T(8,128)(2,1)S(1)}, bf16[16,128]{1,0:T(8,128)(2,1)S(1)}, u32[]{:S(2)}, u32[]{:S(2)}) collective-permute-start(bf16[16,128]{1,0:T(8,128)(2,1)S(1)} %slice_bitcast_fusion.1), channel_id=1, source_target_pairs={{0,64},{8,72},{16,80},{24,88},{32,96},{40,104},{48,112},{56,120},{... | collective-permute-start | bytes 12296 | tf_op jit(solution)/shard_map/ppermute | solution.py:39
  88.6 18.2 %collective-permute-start.8 = (bf16[272,128]{1,0:T(8,128)(2,1)S(1)}, bf16[272,128]{1,0:T(8,128)(2,1)S(1)}, u32[]{:S(2)}, u32[]{:S(2)}) collective-permute-start(bf16[272,128]{1,0:T(8,128)(2,1)S(1)} %get-tuple-element.24), channel_id=1, source_target_pairs={{0,192},{8,200},{16,208},{24,216},{32,224},{40,232},{48,240},{56,2... | collective-permute-start | bytes 208904 | tf_op jit(solution)/shard_map/ppermute | solution.py:39
  89.9 16.9 %collective-permute-start.7 = (bf16[272,128]{1,0:T(8,128)(2,1)S(1)}, bf16[272,128]{1,0:T(8,128)(2,1)S(1)}, u32[]{:S(2)}, u32[]{:S(2)}) collective-permute-start(bf16[272,128]{1,0:T(8,128)(2,1)S(1)} %get-tuple-element.24), channel_id=1, source_target_pairs={{0,128},{8,136},{16,144},{24,152},{32,160},{40,168},{48,176},{56,1... | collective-permute-start | bytes 208904 | tf_op jit(solution)/shard_map/ppermute | solution.py:39
  103.8 3.1 %collective-permute-start.6 = (bf16[272,128]{1,0:T(8,128)(2,1)S(1)}, bf16[272,128]{1,0:T(8,128)(2,1)S(1)}, u32[]{:S(2)}, u32[]{:S(2)}) collective-permute-start(bf16[272,128]{1,0:T(8,128)(2,1)S(1)} %get-tuple-element.24), channel_id=1, source_target_pairs={{0,64},{8,72},{16,80},{24,88},{32,96},{40,104},{48,112},{56,120},{... | collective-permute-start | bytes 208904 | tf_op jit(solution)/shard_map/ppermute | solution.py:39
  105.1 0.7 copy-start.8
  107.1 12.7 %copy-start.1 = (bf16[128,1024]{1,0:T(8,128)(2,1)S(1)}, bf16[128,1024]{1,0:T(8,128)(2,1)}, u32[]{:S(2)}) copy-start(bf16[128,1024]{1,0:T(8,128)(2,1)} %gate.3) | copy-start | bytes 786436
  119.9 3.9 %copy-start.5 = (f32[1024]{0:T(1024)S(1)}, f32[1024]{0:T(1024)}, u32[]{:S(2)}) copy-start(f32[1024]{0:T(1024)} %param.23) | copy-start | bytes 12292
  120.1 3.6 %collective-permute-start.9 = (f32[128,128]{1,0:T(8,128)S(1)}, f32[128,128]{1,0:T(8,128)S(1)}, u32[]{:S(2)}, u32[]{:S(2)}) collective-permute-start(f32[128,128]{1,0:T(8,128)S(1)} %shard_map.124.sums), channel_id=1, source_target_pairs={{0,1},{1,0},{2,3},{3,2},{4,5},{5,4},{6,7},{7,6},{8,9},{9,8},{10,11... | collective-permute-start | bytes 196616 | tf_op jit(solution)/shard_map/ppermute | solution.py:48
